TPU v7x, 32 devices: a whole 2x2x4 slice. The times are simulated.
32 devices in a mesh: group: 2 (over y), tenant: 16 (over z, x, core).
Axes of the slice: x: 2, y: 2, z: 4, core: 2. Of those that a mesh axis runs over, the one named last changes fastest.
Arguments:
- tokens: bfloat16 [4096, 8192], P(('group', 'tenant')), parts along dimension 0, may hold values from -6 to 6
- grad_up: bfloat16 [4096, 16384], P(('group', 'tenant')), parts along dimension 0, may hold values from -6 to 6
- tenant_ids: int32 [4096], P(('group', 'tenant')), parts along dimension 0, may hold values from 0 to 1, as said below
- expert_ids: int32 [4096, 2], P(('group', 'tenant')), parts along dimension 0, may hold values from 0 to 7, as said below
- adapter_down: bfloat16 [16, 16, 8192], P('tenant'), may hold values from -0.0625 to 0.0625
- adapter_up: bfloat16 [16, 16, 16384], P('tenant'), may hold values from -0.046875 to 0.046875
- router: bfloat16 [16, 8192], replicated, may hold values from -0.0625 to 0.0625
Outputs:
- token_grad: bfloat16 [4096, 8192], P(('group', 'tenant')), parts along dimension 0
- grad_down: float32 [32, 16, 8192], P(('group', 'tenant')), parts along dimension 0
- grad_upper: float32 [32, 16, 16384], P(('group', 'tenant')), parts along dimension 0
- router_grad: float32 [32, 8192], P(('group', 'tenant')), parts along dimension 0
There are 2 independent parts, one for each index of `group`. A program takes and returns all parts, laid end to end along the dimension named above; an argument that names none is the same for every part. Nothing has to cross between parts.
Inputs may be any that keep to these rules, and one draw needn't show every extreme that they name: `tenant_ids`: the 128 tokens of one index of tenant form 2 blocks of equal length, one for each tenant, in an order drawn for each index. `expert_ids`: id j of tenant t names expert 8 * t + j, whose factors device 8 * t + j along the mesh axis `tenant` holds. A token's two ids differ. Among the tokens of one index of tenant, every expert is named by exactly 16.
All inputs are finite; a program needn't handle non-finite values.
Results may differ from a plain program's by a relative error of at most 0.0062.
Values may be sent and summed in bfloat16 or wider, within the bound.
A program may use at most 128 MiB of HBM per device.

v0:
```python
import jax
import jax.numpy as jnp
from jax import lax
from jax.sharding import PartitionSpec as P

EXP_TEN = 8


adapter_scale_factor = 2.0


def per_device(tokens, grad_up, tenant_ids, expert_ids, adapter_down, adapter_up, router):
    tok_rows = tokens.shape[0]
    model_width = tokens.shape[1]
    hidden_width = grad_up.shape[1]
    devices = lax.axis_size("tenant")
    capacity = 2 * tok_rows // devices
    buffer_len = devices * capacity
    global_ids = tenant_ids[:, None] * EXP_TEN + expert_ids
    logits = lax.dot_general(
        tokens, router, (((1,), (1,)), ((), ())), preferred_element_type=jnp.float32
    )
    picked = jnp.take_along_axis(logits, global_ids, axis=1)
    first_gate = jax.nn.sigmoid(picked[:, 0] - picked[:, 1])
    gate_sent = jnp.stack([first_gate, 1.0 - first_gate], axis=1).astype(jnp.bfloat16)
    flat_ids = global_ids.reshape(-1)
    slot_count = flat_ids.shape[0]
    same_owner = flat_ids[:, None] == flat_ids[None, :]
    slot_line = jnp.arange(slot_count, dtype=jnp.int32)
    earlier = slot_line[None, :] < slot_line[:, None]
    ranks = jnp.sum((same_owner & earlier).astype(jnp.int32), axis=1)
    places = (flat_ids * capacity + ranks).reshape(tok_rows, 2)

    def spread_rows(values):
        empty = jnp.zeros((buffer_len,) + values.shape[1:], values.dtype)
        return empty.at[places[:, 0]].set(values).at[places[:, 1]].set(values)

    send_rows = spread_rows(tokens).reshape(devices, capacity, model_width)
    send_grads = spread_rows(grad_up).reshape(devices, capacity, hidden_width)
    empty_gates = jnp.zeros((buffer_len,), jnp.bfloat16)
    send_gates = (
        empty_gates.at[places[:, 0]]
        .set(gate_sent[:, 0])
        .at[places[:, 1]]
        .set(gate_sent[:, 1])
        .reshape(devices, capacity)
    )
    recv_rows, recv_grads, recv_gates = (
        lax.all_to_all(send_rows, "tenant", split_axis=0, concat_axis=0, tiled=True),
        lax.all_to_all(send_grads, "tenant", split_axis=0, concat_axis=0, tiled=True),
        lax.all_to_all(send_gates, "tenant", split_axis=0, concat_axis=0, tiled=True),
    )
    rows_in = recv_rows.reshape(buffer_len, model_width)
    grads_in = recv_grads.reshape(buffer_len, hidden_width)
    incoming_gate_values = recv_gates.reshape(buffer_len).astype(jnp.float32)
    down = adapter_down[0]
    upper = adapter_up[0]
    reduced_rank_activations = lax.dot_general(
        rows_in, down, (((1,), (1,)), ((), ())), preferred_element_type=jnp.float32
    )
    returned_rank_gradient = lax.dot_general(
        grads_in, upper, (((1,), (1,)), ((), ())), preferred_element_type=jnp.float32
    )
    position_gate_value = (
        adapter_scale_factor * jnp.sum(reduced_rank_activations * returned_rank_gradient, axis=1)
    ).astype(jnp.bfloat16)
    gate_weighted_output = (
        adapter_scale_factor * incoming_gate_values[:, None] * returned_rank_gradient
    ).astype(jnp.bfloat16)
    scaled_reduced_activations = (
        adapter_scale_factor * incoming_gate_values[:, None] * reduced_rank_activations
    ).astype(jnp.bfloat16)
    slot_rows = jnp.dot(gate_weighted_output, down, preferred_element_type=jnp.float32).astype(
        jnp.bfloat16
    )
    back_rows, back_gates = (
        lax.all_to_all(
            slot_rows.reshape(devices, capacity, model_width),
            "tenant",
            split_axis=0,
            concat_axis=0,
            tiled=True,
        ),
        lax.all_to_all(
            position_gate_value.reshape(devices, capacity),
            "tenant",
            split_axis=0,
            concat_axis=0,
            tiled=True,
        ),
    )
    grad_down = lax.dot_general(
        gate_weighted_output, rows_in, (((0,), (0,)), ((), ())), preferred_element_type=jnp.float32
    )
    grad_upper = lax.dot_general(
        scaled_reduced_activations,
        grads_in,
        (((0,), (0,)), ((), ())),
        preferred_element_type=jnp.float32,
    )
    flat_back = back_rows.reshape(buffer_len, model_width)
    expert_grad = flat_back[places[:, 0]].astype(jnp.float32) + flat_back[places[:, 1]].astype(
        jnp.float32
    )
    gate_grads = back_gates.reshape(buffer_len)[places].astype(jnp.float32)
    logit_grad = first_gate * (1.0 - first_gate) * (gate_grads[:, 0] - gate_grads[:, 1])
    logit_sent = logit_grad.astype(jnp.bfloat16)
    columns = jnp.arange(router.shape[0], dtype=jnp.int32)[None, :]
    nothing = jnp.zeros((), jnp.bfloat16)
    signed = jnp.where(columns == global_ids[:, 0:1], logit_sent[:, None], nothing) - jnp.where(
        columns == global_ids[:, 1:2], logit_sent[:, None], nothing
    )
    router_term = jnp.dot(signed, router, preferred_element_type=jnp.float32)
    token_grad = (expert_grad + router_term).astype(jnp.bfloat16)
    router_grad = lax.psum_scatter(
        lax.dot_general(
            signed, tokens, (((0,), (0,)), ((), ())), preferred_element_type=jnp.float32
        ),
        "tenant",
        scatter_dimension=0,
        tiled=True,
    )
    return (token_grad, grad_down[None], grad_upper[None], router_grad)


def solution(mesh):
    in_specs = (
        P(("group", "tenant"), None),
        P(("group", "tenant"), None),
        P(("group", "tenant")),
        P(("group", "tenant"), None),
        P("tenant", None, None),
        P("tenant", None, None),
        P(),
    )
    out_specs = (
        P(("group", "tenant"), None),
        P(("group", "tenant"), None, None),
        P(("group", "tenant"), None, None),
        P(("group", "tenant"), None),
    )
    return jax.shard_map(
        per_device, mesh=mesh, in_specs=in_specs, out_specs=out_specs, check_vma=False
    )
```

profile of v0, /device:TPU:0, one launch (start us, length us, event | category | flops | bytes accessed | tf_op | source)
XLA Modules:
  0.0 541.8 jit_solution(13416567475755950)
XLA Ops:
  7.2 0.7 broadcast_multiply_fusion
  7.9 0.7 bitcast_or_fusion
  8.6 0.1 copy.19
  8.7 0.1 eq.45
  8.8 0.2 convert_reduce_fusion
  9.0 0.1 reduce_sum.21
  9.3 12.7 %scatter_custom_fusion.2 = bf16[256,16384]{1,0:T(8,128)(2,1)} fusion(s32[128]{0:T(128)S(1)} %get-tuple-element.15, bf16[128,16384]{1,0:T(8,128)(2,1)} %param.8, bf16[]{:T(256)} %constant.10.clone.1), kind=kCustom, calls=%fused_computation.15 | custom fusion | bytes 8389120 | tf_op jit(solution)/shard_map/scatter | solution.py:36
  21.9 15.6 %scatter_fusion.1 = bf16[256,16384]{1,0:T(8,128)(2,1)} fusion(bf16[256,16384]{1,0:T(8,128)(2,1)} %scatter_custom_fusion.2, s32[128]{0:T(128)S(1)} %get-tuple-element.14, bf16[128,16384]{1,0:T(8,128)(2,1)} %param.8), kind=kCustom, calls=%fused_computation.7 | custom fusion | bytes 12583424 | tf_op jit(solution)/shard_map/scatter | solution.py:36
  37.5 7.7 %all-to-all-start.1 = ((bf16[16,16,16384]{2,1,0:T(8,128)(2,1)}), bf16[16,16,16384]{2,1,0:T(8,128)(2,1)}, u32[]{:S(2)}, u32[]{:S(2)}) async-start(bf16[16,16,16384]{2,1,0:T(8,128)(2,1)} %bitcast.47), calls=%async_computation.1 | async-start | bytes 16777216 | tf_op jit(solution)/shard_map/all_to_all | solution.py:50
  45.3 6.0 %scatter_custom_fusion.4 = bf16[256,8192]{1,0:T(8,128)(2,1)} fusion(s32[128]{0:T(128)S(1)} %get-tuple-element.15, bf16[128,8192]{1,0:T(8,128)(2,1)S(1)} %copy-done.1, bf16[]{:T(256)} %constant.10.clone.1), kind=kCustom, calls=%fused_computation.17 | custom fusion | bytes 4194306 | tf_op jit(solution)/shard_map/scatter | solution.py:36
  51.2 8.1 %scatter_fusion.2 = bf16[256,8192]{1,0:T(8,128)(2,1)} fusion(bf16[256,8192]{1,0:T(8,128)(2,1)} %scatter_custom_fusion.4, s32[128]{0:T(128)S(1)} %get-tuple-element.14, bf16[128,8192]{1,0:T(8,128)(2,1)S(1)} %copy-done.1), kind=kCustom, calls=%fused_computation.9 | custom fusion | bytes 6291968 | tf_op jit(solution)/shard_map/scatter | solution.py:36
  59.4 136.6 %all-to-all-done.1 = bf16[16,16,16384]{2,1,0:T(8,128)(2,1)} async-done(((bf16[16,16,16384]{2,1,0:T(8,128)(2,1)}), bf16[16,16,16384]{2,1,0:T(8,128)(2,1)}, u32[]{:S(2)}, u32[]{:S(2)}) %all-to-all-start.1) | async-done | bytes 8388640 | tf_op jit(solution)/shard_map/all_to_all | solution.py:50
  196.0 36.9 %all-to-all-start.3 = ((bf16[16,16,8192]{2,1,0:T(8,128)(2,1)}), bf16[16,16,8192]{2,1,0:T(8,128)(2,1)}, u32[]{:S(2)}, u32[]{:S(2)}) async-start(bf16[16,16,8192]{2,1,0:T(8,128)(2,1)} %bitcast.48), calls=%async_computation.3 | async-start | bytes 8388608 | tf_op jit(solution)/shard_map/all_to_all | solution.py:49
  232.9 0.1 copy.25
  233.0 0.1 reshape.108
  233.1 0.1 copy.21
  233.2 0.1 reshape.114
  233.4 0.6 fusion.27
  234.0 2.0 gather_fusion.3
  236.0 0.1 reshape.117
  236.3 5.7 %fusion.5 = f32[256,16]{0,1:T(8,128)S(1)} fusion(bf16[256,16384]{1,0:T(8,128)(2,1)} %bitcast.6, bf16[1,16,16384]{2,1,0:T(8,128)(2,1)S(1)} %copy-done), kind=kOutput, calls=%fused_computation.19 | convolution fusion | flops 134217728 | bytes 8929280 | tf_op jit(solution)/shard_map/dot_general | solution.py:61
  241.9 68.6 %all-to-all-done.3 = bf16[16,16,8192]{2,1,0:T(8,128)(2,1)} async-done(((bf16[16,16,8192]{2,1,0:T(8,128)(2,1)}), bf16[16,16,8192]{2,1,0:T(8,128)(2,1)}, u32[]{:S(2)}, u32[]{:S(2)}) %all-to-all-start.3) | async-done | bytes 4194336 | tf_op jit(solution)/shard_map/all_to_all | solution.py:49
  310.5 3.4 multiply_reduce_fusion
  313.9 0.7 convert_element_type.64
  314.6 19.6 %all-to-all-start.4 = ((bf16[16,1,16]{2,1,0:T(2,128)(2,1)}), bf16[16,1,16]{2,1,0:T(2,128)(2,1)S(1)}, u32[]{:S(2)}, u32[]{:S(2)}) async-start(bf16[16,1,16]{2,1,0:T(2,128)(2,1)} %convert_element_type.64), calls=%async_computation.4 | async-start | bytes 16384 | tf_op jit(solution)/shard_map/all_to_all | solution.py:84
  334.3 6.3 %all-to-all-done.4 = bf16[16,1,16]{2,1,0:T(2,128)(2,1)S(1)} async-done(((bf16[16,1,16]{2,1,0:T(2,128)(2,1)}), bf16[16,1,16]{2,1,0:T(2,128)(2,1)S(1)}, u32[]{:S(2)}, u32[]{:S(2)}) %all-to-all-start.4) | async-done | bytes 544 | tf_op jit(solution)/shard_map/all_to_all | solution.py:84
  340.6 0.1 reshape.89
  340.7 1.9 gather_fusion.2
  342.6 0.1 reshape.170
  342.7 0.1 fusion.26
  342.9 0.1 copy.29
  343.0 1.3 scatter_custom_fusion
  344.4 1.3 scatter_fusion
  345.7 0.1 all_to_all.25
  345.8 9.0 %all_to_all.31 = bf16[16,1,16]{2,1,0:T(2,128)(2,1)S(1)} all-to-all(bf16[16,1,16]{2,1,0:T(2,128)(2,1)S(1)} %all_to_all.25), channel_id=1, replica_groups=mesh['group'=2,'tenant'=16] {'tenant'}, dimensions={0} | all-to-all | bytes 1024 | tf_op jit(solution)/shard_map/all_to_all | solution.py:51
  354.8 0.1 mul.71
  354.9 3.2 convolution_convert_fusion
  358.2 4.7 all-to-all-start.2
  362.8 0.3 all-reduce.3.cloned.1.call-start
  363.2 0.6 dynamic-slice
  363.8 1.3 fusion.14
  365.2 5.6 %convolution_bitcast_fusion = f32[1,16,16384]{2,1,0:T(8,128)} fusion(bf16[256,16384]{1,0:T(8,128)(2,1)} %bitcast.6, f32[256,16]{0,1:T(8,128)S(1)} %get-tuple-element.19, f32[256]{0:T(256)S(1)} %mul.71), kind=kOutput, calls=%fused_computation.10 | convolution fusion | flops 134225920 | bytes 9454592 | tf_op jit(solution)/shard_map/dot_general | solution.py:95
  370.7 3.6 convolution_bitcast_fusion.1
  374.4 139.9 %all-reduce.3.cloned.1.call-done = f32[16,8192]{1,0:T(8,128)} async-done(((f32[16,8192]{1,0:T(8,128)}), f32[16,8192]{1,0:T(8,128)}) %all-reduce.3.cloned.1.call-update) | async-done | bytes 524304
  514.3 2.2 constant_dynamic-slice_fusion
  516.5 6.5 %gather_fusion = bf16[128,8192]{1,0:T(8,128)(2,1)S(1)} fusion(bf16[256,8192]{1,0:T(8,128)(2,1)} %bitcast.10, s32[1024]{0:T(1024)S(1)} %get-tuple-element.21), kind=kCustom, calls=%fused_computation | custom fusion | bytes 4194816 | tf_op jit(solution)/shard_map/gather | solution.py:102
  523.0 7.8 %gather_fusion.1 = bf16[128,8192]{1,0:T(8,128)(2,1)} fusion(bf16[256,8192]{1,0:T(8,128)(2,1)} %bitcast.10, s32[1024]{0:T(1024)S(1)} %get-tuple-element.20), kind=kCustom, calls=%fused_computation.1 | custom fusion | bytes 4194816 | tf_op jit(solution)/shard_map/gather | solution.py:102
  530.8 3.7 fusion
  (26 shorter events, 0.4 us)
Async XLA Ops:
  7.2 229.1 %copy-start = (bf16[1,16,16384]{2,1,0:T(8,128)(2,1)S(1)}, bf16[1,16,16384]{2,1,0:T(8,128)(2,1)}, u32[]{:S(2)}) copy-start(bf16[1,16,16384]{2,1,0:T(8,128)(2,1)} %param.12) | copy-start | bytes 1572868
  37.5 7.7 %copy-start.1 = (bf16[128,8192]{1,0:T(8,128)(2,1)S(1)}, bf16[128,8192]{1,0:T(8,128)(2,1)}, u32[]{:S(2)}) copy-start(bf16[128,8192]{1,0:T(8,128)(2,1)} %param.7) | copy-start | bytes 6291460
  37.5 158.4 %all-to-all-start.1 = ((bf16[16,16,16384]{2,1,0:T(8,128)(2,1)}), bf16[16,16,16384]{2,1,0:T(8,128)(2,1)}, u32[]{:S(2)}, u32[]{:S(2)}) async-start(bf16[16,16,16384]{2,1,0:T(8,128)(2,1)} %bitcast.47), calls=%async_computation.1 | async-start | bytes 16777216 | tf_op jit(solution)/shard_map/all_to_all | solution.py:50
  196.0 37.4 %copy-start.3 = (bf16[16,8192]{1,0:T(8,128)(2,1)S(1)}, bf16[16,8192]{1,0:T(8,128)(2,1)}, u32[]{:S(2)}) copy-start(bf16[16,8192]{1,0:T(8,128)(2,1)} %param.13) | copy-start | bytes 786436
  196.0 114.6 %all-to-all-start.3 = ((bf16[16,16,8192]{2,1,0:T(8,128)(2,1)}), bf16[16,16,8192]{2,1,0:T(8,128)(2,1)}, u32[]{:S(2)}, u32[]{:S(2)}) async-start(bf16[16,16,8192]{2,1,0:T(8,128)(2,1)} %bitcast.48), calls=%async_computation.3 | async-start | bytes 8388608 | tf_op jit(solution)/shard_map/all_to_all | solution.py:49
  236.3 74.3 %copy-start.2 = (bf16[1,16,8192]{2,1,0:T(8,128)(2,1)S(1)}, bf16[1,16,8192]{2,1,0:T(8,128)(2,1)}, u32[]{:S(2)}) copy-start(bf16[1,16,8192]{2,1,0:T(8,128)(2,1)} %param.11) | copy-start | bytes 786436
  314.6 26.0 %all-to-all-start.4 = ((bf16[16,1,16]{2,1,0:T(2,128)(2,1)}), bf16[16,1,16]{2,1,0:T(2,128)(2,1)S(1)}, u32[]{:S(2)}, u32[]{:S(2)}) async-start(bf16[16,1,16]{2,1,0:T(2,128)(2,1)} %convert_element_type.64), calls=%async_computation.4 | async-start | bytes 16384 | tf_op jit(solution)/shard_map/all_to_all | solution.py:84
  358.2 5.0 copy-start.4
  358.2 158.4 %all-to-all-start.2 = ((bf16[16,16,8192]{2,1,0:T(8,128)(2,1)}), bf16[16,16,8192]{2,1,0:T(8,128)(2,1)}, u32[]{:S(2)}, u32[]{:S(2)}) async-start(bf16[16,16,8192]{2,1,0:T(8,128)(2,1)} %bitcast.49), calls=%async_computation.2 | async-start | bytes 8388608 | tf_op jit(solution)/shard_map/all_to_all | solution.py:77
  362.8 151.5 %all-reduce.3.cloned.1.call-start = ((), (), s32[]{:S(2)}) async-start(), calls=%async_computation.5 | async-start | bytes 1048576
Sparse Core Ops, SparseCore 0:
  367.7 146.6 all-reduce.2
where the time goes:
time: 550 us; the launch traced here: 542 us
  waiting for transfers between devices  351 us (64%)
  starting transfers between devices  69.2 us (13%)
  local copies, waits for them, and re-layouts  68.6 us (12%)
  matrix products  27.2 us (5%)
  between operations  14.7 us (3%)
  blocking collectives  8.97 us (2%)
    unnamed x2, waiting for transfers between devices  140 us
    all_to_all x1, waiting for transfers between devices, per_device(): lax.all_to_all(send_grads, 'tenant', split_axis=0, concat_axis=0, tiled=T...  137 us
    all_to_all x1, waiting for transfers between devices, per_device(): lax.all_to_all(send_rows, 'tenant', split_axis=0, concat_axis=0, tiled=True)  68.6 us
    scatter x4, local copies, waits for them, and re-layouts, spread_rows(): return empty.at[places[:, 0]].set(values).at[places[:, 1]].set(values)  42.4 us
    all_to_all x1, starting transfers between devices, per_device(): lax.all_to_all(send_rows, 'tenant', split_axis=0, concat_axis=0, tiled=True)  36.9 us
    all_to_all x1, starting transfers between devices, per_device(): lax.all_to_all(position_gate_value.reshape(devices, capacity), 'tenant',...  19.6 us
  transfers between devices with their start and end apart: 5, of which 4 were waited for; matrix products, arithmetic and copies ran while one was open for 7% of the time, Pallas kernels for 0%

commit v1 on v0

--- a/solution.py
+++ b/solution.py
@@ -7,9 +7,10 @@
 
 
 adapter_scale_factor = 2.0
-
-
-def per_device(tokens, grad_up, tenant_ids, expert_ids, adapter_down, adapter_up, router):
+SUM_TYPE = jnp.bfloat16
+
+
+def routed(tokens, grad_up, tenant_ids, expert_ids, adapter_down, adapter_up, router):
     tok_rows = tokens.shape[0]
     model_width = tokens.shape[1]
     hidden_width = grad_up.shape[1]
@@ -123,6 +124,61 @@
     return (token_grad, grad_down[None], grad_upper[None], router_grad)
 
 
+GATHER_LIMIT = 16 * 1024 * 1024
+
+
+def gathered(tokens, grad_up, tenant_ids, expert_ids, adapter_down, adapter_up, router):
+    tok_rows = tokens.shape[0]
+    experts = lax.axis_size("tenant")
+    rank = adapter_down.shape[1]
+    upper = lax.all_gather(adapter_up[0], "tenant", axis=0, tiled=True)
+    down = lax.all_gather(adapter_down[0], "tenant", axis=0, tiled=True)
+    global_ids = tenant_ids[:, None] * EXP_TEN + expert_ids
+    columns = jnp.arange(experts, dtype=jnp.int32)[None, :]
+    first_hot = columns == global_ids[:, 0:1]
+    second_hot = columns == global_ids[:, 1:2]
+    sign = first_hot.astype(jnp.float32) - second_hot.astype(jnp.float32)
+    nt = (((1,), (1,)), ((), ()))
+    tn = (((0,), (0,)), ((), ()))
+    logits = lax.dot_general(tokens, router, nt, preferred_element_type=jnp.float32)
+    first_gate = jax.nn.sigmoid(jnp.sum(logits * sign, axis=1, keepdims=True))
+    gates = jnp.where(first_hot, first_gate, 0.0) + jnp.where(second_hot, 1.0 - first_gate, 0.0)
+    gates = gates.astype(jnp.bfloat16).astype(jnp.float32)
+    wide_gates = adapter_scale_factor * jnp.repeat(gates, rank, axis=1)
+    back = lax.dot_general(grad_up, upper, nt, preferred_element_type=jnp.float32)
+    low = lax.dot_general(tokens, down, nt, preferred_element_type=jnp.float32)
+    weighted = (wide_gates * back).astype(jnp.bfloat16)
+    scaled = (wide_gates * low).astype(jnp.bfloat16)
+    slot_gate = adapter_scale_factor * jnp.sum((low * back).reshape(tok_rows, experts, rank), axis=2)
+    slot_gate = slot_gate.astype(jnp.bfloat16).astype(jnp.float32)
+    slot_diff = jnp.sum(slot_gate * sign, axis=1, keepdims=True)
+    logit_sent = (first_gate * (1.0 - first_gate) * slot_diff).astype(jnp.bfloat16)
+    signed = (logit_sent.astype(jnp.float32) * sign).astype(jnp.bfloat16)
+    down_part = lax.dot_general(weighted, tokens, tn, preferred_element_type=jnp.float32)
+    upper_part = lax.dot_general(scaled, grad_up, tn, preferred_element_type=jnp.float32)
+    router_part = lax.dot_general(signed, tokens, tn, preferred_element_type=jnp.float32)
+
+    def reduce(part):
+        return lax.psum_scatter(
+            part.astype(SUM_TYPE), "tenant", scatter_dimension=0, tiled=True
+        ).astype(jnp.float32)
+
+    grad_upper = reduce(upper_part)
+    grad_down = reduce(down_part)
+    router_grad = lax.psum_scatter(router_part, "tenant", scatter_dimension=0, tiled=True)
+    token_grad = (
+        jnp.dot(weighted, down, preferred_element_type=jnp.float32)
+        + jnp.dot(signed, router, preferred_element_type=jnp.float32)
+    ).astype(jnp.bfloat16)
+    return (token_grad, grad_down[None], grad_upper[None], router_grad)
+
+
+def per_device(tokens, grad_up, tenant_ids, expert_ids, adapter_down, adapter_up, router):
+    factor_bytes = 2 * (adapter_down.size + adapter_up.size)
+    plan = gathered if lax.axis_size("tenant") * factor_bytes <= GATHER_LIMIT else routed
+    return plan(tokens, grad_up, tenant_ids, expert_ids, adapter_down, adapter_up, router)
+
+
 def solution(mesh):
     in_specs = (
         P(("group", "tenant"), None),

time: 550 us -> 427 us (0.78); the launches traced: 542 us -> 426 us
  starting transfers between devices: 69.2 us -> 0.2 us
  local copies, waits for them, and re-layouts: 68.6 us -> 3.66 us
  waiting for transfers between devices: 351 us -> 373 us
  blocking collectives: 8.97 us -> 0 us
    all_to_all x4 -> x0, waiting for transfers between devices: 211 us -> none  [the longest x1 137 us: per_device(): lax.all_to_all(send_grads, 'tenant', split_axis=0, concat_axis=0, tiled=T...]
    reduce_scatter x0 -> x2, waiting for transfers between devices: none -> 181 us  [reduce(): lax.psum_scatter(part.astype(SUM_TYPE), 'tenant', scatter_dimension=0, ti...]
    all_gather x0 -> x2, waiting for transfers between devices: none -> 120 us  [the longest x1 76.1 us: gathered(): upper = lax.all_gather(adapter_up[0], 'tenant', axis=0, tiled=True)]
    all_to_all x4 -> x0, starting transfers between devices: 68.9 us -> none  [the longest x1 36.9 us: per_device(): lax.all_to_all(send_rows, 'tenant', split_axis=0, concat_axis=0, tiled=True)]
    unnamed x2 -> x6, waiting for transfers between devices: 140 us -> 72.7 us
    scatter x6 -> x0, local copies, waits for them, and re-layouts: 45.1 us -> none  [the longest x4 42.4 us: spread_rows(): return empty.at[places[:, 0]].set(values).at[places[:, 1]].set(values)]
    gather x8 -> x0, local copies, waits for them, and re-layouts: 18.6 us -> none  [the longest x1 7.81 us: per_device(): flat_back[places[:, 1]].astype(jnp.float32)]
    all_to_all x1 -> x0, blocking collectives: 8.97 us -> none  [per_device(): lax.all_to_all(send_gates, 'tenant', split_axis=0, concat_axis=0, tiled=T...]
  transfers between devices with their start and end apart: 5 -> 5, of which waited for: 4 -> 5; matrix products, arithmetic and copies ran while one was open for 7% -> 7% of each run, Pallas kernels for 0% -> 0%
where the time goes in v1:
time: 427 us; the launch traced here: 426 us
  waiting for transfers between devices  373 us (87%)
  matrix products  30.1 us (7%)
  between operations  13.9 us (3%)
  other arithmetic  5.29 us (1%)
    reduce_scatter x2, waiting for transfers between devices, reduce(): lax.psum_scatter(part.astype(SUM_TYPE), 'tenant', scatter_dimension=0, ti...  181 us
    all_gather x1, waiting for transfers between devices, gathered(): upper = lax.all_gather(adapter_up[0], 'tenant', axis=0, tiled=True)  76.1 us
    unnamed x6, waiting for transfers between devices  72.7 us
    all_gather x1, waiting for transfers between devices, gathered(): down = lax.all_gather(adapter_down[0], 'tenant', axis=0, tiled=True)  43.4 us
  transfers between devices with their start and end apart: 5, of which 5 were waited for; matrix products, arithmetic and copies ran while one was open for 7% of the time, Pallas kernels for 0%

profile of v1, /device:TPU:0, one launch (start us, length us, event | category | flops | bytes accessed | tf_op | source)
XLA Modules:
  0.0 426.3 jit_solution(16476083563460295612)
XLA Ops:
  7.2 0.0 copy-start
  7.2 0.0 all-gather.5.cloned.1.call-start
  7.2 0.7 all-gather.5.cloned.1.call-update
  7.9 0.0 all-gather.7.cloned.1.call-start
  8.0 0.7 all-gather.7.cloned.1.call-update
  8.7 0.0 all-reduce.3.cloned.1.call-start
  8.7 0.7 broadcast_multiply_fusion
  9.4 0.7 broadcast_add_fusion
  10.1 0.0 copy-done
  10.1 1.6 fusion.7
  11.7 76.1 %all-gather.5.cloned.1.call-done = bf16[1,256,16384]{2,1,0:T(8,128)(2,1)} async-done(((bf16[1,16,16384]{2,1,0:T(8,128)(2,1)}), bf16[1,256,16384]{2,1,0:T(8,128)(2,1)}) %all-gather.5.cloned.1.call-update) | async-done | bytes 8388624 | tf_op jit(solution)/shard_map/all_gather | solution.py:134
  87.8 7.6 %fusion.1 = f32[128,256]{1,0:T(8,128)S(1)} fusion(bf16[128,16384]{1,0:T(8,128)(2,1)} %param.8, bf16[1,256,16384]{2,1,0:T(8,128)(2,1)} %all-gather.5.cloned.1.call-done), kind=kOutput, calls=%fused_computation.4 | convolution fusion | flops 1073741824 | bytes 12713984 | tf_op jit(solution)/shard_map/dot_general | solution.py:148
  95.4 43.4 %all-gather.7.cloned.1.call-done = bf16[1,256,8192]{2,1,0:T(8,128)(2,1)} async-done(((bf16[1,16,8192]{2,1,0:T(8,128)(2,1)}), bf16[1,256,8192]{2,1,0:T(8,128)(2,1)}) %all-gather.7.cloned.1.call-update) | async-done | bytes 4194320 | tf_op jit(solution)/shard_map/all_gather | solution.py:135
  138.8 3.7 fusion.15
  142.5 0.1 copy.16
  142.7 0.1 copy.15
  142.9 1.2 fusion.8
  144.1 0.0 all-reduce.3.cloned.1.call-update
  144.1 0.0 reduce-scatter.3.cloned.1.call-start
  144.1 3.2 convolution_convert_fusion.1
  147.3 0.0 reduce-scatter.3.cloned.1.call-update
  147.4 0.0 reduce-scatter.5.cloned.1.call-start
  147.4 7.8 %convolution_convert_fusion = bf16[256,16384]{1,0:T(8,128)(2,1)} fusion(bf16[128,16384]{1,0:T(8,128)(2,1)} %param.8, f32[128,256]{1,0:T(8,128)S(1)} %copy.15, f32[128,256]{1,0:T(8,128)S(1)} %get-tuple-element.9), kind=kOutput, calls=%fused_computation | convolution fusion | flops 1078001664 | bytes 12845056 | tf_op jit(solution)/shard_map/dot_general | solution.py:158
  155.2 0.0 copy-start.2
  155.2 0.0 reduce-scatter.5.cloned.1.call-update
  155.3 0.6 copy-done.2
  155.9 0.6 dynamic-slice
  156.5 0.0 copy-start.1
  156.5 3.0 fusion.5
  159.4 0.0 copy-done.1
  159.5 2.1 fusion
  161.5 71.3 %all-reduce.3.cloned.1.call-done = f32[16,8192]{1,0:T(8,128)} async-done(((f32[16,8192]{1,0:T(8,128)}), f32[16,8192]{1,0:T(8,128)}) %all-reduce.3.cloned.1.call-update) | async-done | bytes 524304
  232.8 2.2 constant_dynamic-slice_fusion
  235.0 74.3 %reduce-scatter.3.cloned.1.call-done = bf16[16,8192]{1,0:T(8,128)(2,1)} async-done(((bf16[256,8192]{1,0:T(8,128)(2,1)}), bf16[16,8192]{1,0:T(8,128)(2,1)}) %reduce-scatter.3.cloned.1.call-update) | async-done | bytes 262160 | tf_op jit(solution)/shard_map/reduce_scatter | solution.py:162
  309.4 1.8 bitcast_convert_fusion.1
  311.1 106.5 %reduce-scatter.5.cloned.1.call-done = bf16[16,16384]{1,0:T(8,128)(2,1)} async-done(((bf16[256,16384]{1,0:T(8,128)(2,1)}), bf16[16,16384]{1,0:T(8,128)(2,1)}) %reduce-scatter.5.cloned.1.call-update) | async-done | bytes 524304 | tf_op jit(solution)/shard_map/reduce_scatter | solution.py:162
  417.7 2.1 bitcast_convert_fusion
  (8 shorter events, 0.1 us)
Async XLA Ops:
  7.2 2.9 copy-start
  7.2 80.6 %all-gather.5.cloned.1.call-start = ((), (), s32[]{:S(2)}) async-start(), calls=%async_computation.4 | async-start | bytes 8912896 | tf_op jit(solution)/shard_map/all_gather | solution.py:134
  7.9 130.9 %all-gather.7.cloned.1.call-start = ((), (), s32[]{:S(2)}) async-start(), calls=%async_computation.5 | async-start | bytes 4456448 | tf_op jit(solution)/shard_map/all_gather | solution.py:135
  8.7 224.1 %all-reduce.3.cloned.1.call-start = ((), (), s32[]{:S(2)}) async-start(), calls=%async_computation.6 | async-start | bytes 1048576
  144.1 165.3 %reduce-scatter.3.cloned.1.call-start = ((), (), s32[]{:S(2)}) async-start(), calls=%async_computation.2 | async-start | bytes 4456448 | tf_op jit(solution)/shard_map/reduce_scatter | solution.py:162
  147.4 270.3 %reduce-scatter.5.cloned.1.call-start = ((), (), s32[]{:S(2)}) async-start(), calls=%async_computation.3 | async-start | bytes 8912896 | tf_op jit(solution)/shard_map/reduce_scatter | solution.py:162
  155.2 0.7 copy-start.2
  156.5 3.0 copy-start.1
Sparse Core Ops, SparseCore 0:
  10.2 77.5 all-gather.4
  90.0 48.8 all-gather.6
  144.2 88.5 all-reduce.2
  236.5 72.7 reduce-scatter.2
  313.8 103.7 reduce-scatter.4

commit v2 on v0

--- a/solution.py
+++ b/solution.py
@@ -1,6 +1,10 @@
 import jax
 import jax.numpy as jnp
+import functools
+
 from jax import lax
+from jax.experimental import pallas as pl
+from jax.experimental.pallas import tpu as pltpu
 from jax.sharding import PartitionSpec as P
 
 EXP_TEN = 8
@@ -9,7 +13,7 @@
 adapter_scale_factor = 2.0
 
 
-def per_device(tokens, grad_up, tenant_ids, expert_ids, adapter_down, adapter_up, router):
+def routed(tokens, grad_up, tenant_ids, expert_ids, adapter_down, adapter_up, router):
     tok_rows = tokens.shape[0]
     model_width = tokens.shape[1]
     hidden_width = grad_up.shape[1]
@@ -123,6 +127,400 @@
     return (token_grad, grad_down[None], grad_upper[None], router_grad)
 
 
+F32 = jnp.float32
+BF16 = jnp.bfloat16
+TILE = 1024
+PIECE = 512
+
+
+def loop(count, body):
+    def step(i, carry):
+        body(i)
+        return carry
+
+    lax.fori_loop(0, count, step, 0)
+
+
+def fused_kernel(
+    tok, gup, ids, adn, aup, router,
+    tok_out, dn_out, up_out, rt_out,
+    fac, part, core_in, x_in, left_in, right_in,
+    low, back, logits, wide, wide_t, scaled_t, sign_t, signed, acc,
+    own_sem, ag_send, ag_recv, core_send, core_recv, x_send, x_recv, z_send, left_recv, right_recv,
+):
+    me = lax.axis_index("tenant")
+    c = lax.rem(me, 2)
+    x = lax.rem(lax.div(me, 2), 2)
+    z = lax.div(me, 4)
+    model = tok.shape[1]
+    hidden = gup.shape[1]
+    both = model + hidden
+    total = part.shape[2]
+    rows = tok.shape[0]
+
+    right = me + 4
+    left = me - 4
+    x_peer = me + 2 - 4 * x
+    c_peer = me + 1 - 2 * c
+
+    def slot(cc, zz, xx):
+        return cc * 8 + zz * 2 + xx
+
+    barrier = pltpu.get_barrier_semaphore()
+
+    def greet(peer):
+        pl.semaphore_signal(
+            barrier, inc=1, device_id={"tenant": peer}, device_id_type=pl.DeviceIdType.MESH
+        )
+
+    own = slot(c, z, x)
+    own_dn = pltpu.make_async_copy(adn, fac.at[own, :, pl.ds(0, model)], own_sem.at[0])
+    own_up = pltpu.make_async_copy(aup, fac.at[own, :, pl.ds(model, hidden)], own_sem.at[1])
+    own_dn.start()
+    own_up.start()
+    greet(x_peer)
+    greet(c_peer)
+    pl.when(z < 3)(lambda: greet(right))
+    pl.when(z > 0)(lambda: greet(left))
+    pl.semaphore_wait(
+        barrier, 2 + jnp.where(z < 3, 1, 0).astype(jnp.int32) + jnp.where(z > 0, 1, 0).astype(jnp.int32)
+    )
+    own_dn.wait()
+    own_up.wait()
+
+    def remote(src, dst, send, recv, peer):
+        return pltpu.make_async_remote_copy(
+            src_ref=src, dst_ref=dst, send_sem=send, recv_sem=recv,
+            device_id={"tenant": peer}, device_id_type=pl.DeviceIdType.MESH,
+        )
+
+    def gather_copy(at, send_at, peer):
+        return remote(fac.at[at], fac.at[at], ag_send.at[send_at], ag_recv.at[at], peer)
+
+    def to_right(zz):
+        return gather_copy(slot(c, zz, x), zz, right)
+
+    def to_left(zz):
+        return gather_copy(slot(c, zz, x), 4 + zz, left)
+
+    def to_x(zz):
+        return gather_copy(slot(c, zz, x), 8 + zz, x_peer)
+
+    def to_core(zz, xx):
+        return gather_copy(slot(c, zz, xx), 12 + zz * 2 + xx, c_peer)
+
+    def arrived(at):
+        gather_copy(at, 0, c_peer).wait_recv()
+
+    pl.when(z < 3)(lambda: to_right(z).start())
+    pl.when(z > 0)(lambda: to_left(z).start())
+    to_x(z).start()
+    to_core(z, x).start()
+
+    nt = (((1,), (1,)), ((), ()))
+    logits[...] = jnp.zeros_like(logits)
+
+    def logit_tile(i):
+        cols = pl.ds(pl.multiple_of(i * TILE, TILE), TILE)
+        logits[...] += lax.dot_general(tok[:, cols], router[:, cols], nt, preferred_element_type=F32)
+
+    loop(model // TILE, logit_tile)
+
+    for s in range(1, 4):
+        def from_left(s=s):
+            arrived(slot(c, z - s, x))
+            pl.when(z < 3)(lambda: to_right(z - s).start())
+            to_x(z - s).start()
+            to_core(z - s, x).start()
+
+        def from_right(s=s):
+            arrived(slot(c, z + s, x))
+            pl.when(z > 0)(lambda: to_left(z + s).start())
+            to_x(z + s).start()
+            to_core(z + s, x).start()
+
+        pl.when(z - s >= 0)(from_left)
+        pl.when(z + s <= 3)(from_right)
+
+    def x_block(zz):
+        arrived(slot(c, zz, 1 - x))
+        to_core(zz, 1 - x).start()
+
+    x_block(z)
+    for s in range(1, 4):
+        pl.when(z - s >= 0)(functools.partial(x_block, z - s))
+        pl.when(z + s <= 3)(functools.partial(x_block, z + s))
+    for k in range(8):
+        arrived((1 - c) * 8 + k)
+
+    def factor_tile(start):
+        return fac[:, :, pl.ds(start, TILE)].reshape(256, TILE)
+
+    low[...] = jnp.zeros_like(low)
+    back[...] = jnp.zeros_like(back)
+
+    def low_tile(i):
+        start = pl.multiple_of(i * TILE, TILE)
+        low[...] += lax.dot_general(
+            tok[:, pl.ds(start, TILE)], factor_tile(start), nt, preferred_element_type=F32
+        )
+
+    def back_tile(i):
+        start = pl.multiple_of(i * TILE, TILE)
+        back[...] += lax.dot_general(
+            gup[:, pl.ds(start, TILE)],
+            factor_tile(pl.multiple_of(model + start, TILE)),
+            nt,
+            preferred_element_type=F32,
+        )
+
+    loop(model // TILE, low_tile)
+    loop(hidden // TILE, back_tile)
+
+    first = ids[:, 0:1]
+    second = ids[:, 1:2]
+    narrow = lax.broadcasted_iota(jnp.int32, (rows, 16), 1)
+    n_sign = jnp.where(narrow == first, 1.0, 0.0) - jnp.where(narrow == second, 1.0, 0.0)
+    first_gate = jax.nn.sigmoid(jnp.sum(logits[...] * n_sign, axis=1, keepdims=True))
+    place = lax.broadcasted_iota(jnp.int32, (rows, 256), 1) // 16
+    expert = (place % 8) * 2 + place // 8
+    hot1 = expert == first
+    hot2 = expert == second
+    one = first_gate.astype(BF16).astype(F32)
+    two = (1.0 - first_gate).astype(BF16).astype(F32)
+    gates = adapter_scale_factor * (jnp.where(hot1, one, 0.0) + jnp.where(hot2, two, 0.0))
+    lows = low[...]
+    backs = back[...]
+    weighted = gates * backs
+    product = lows * backs
+
+    def slot_gate(hot):
+        picked = jnp.sum(jnp.where(hot, product, 0.0), axis=1, keepdims=True)
+        return (adapter_scale_factor * picked).astype(BF16).astype(F32)
+
+    logit_sent = first_gate * (1.0 - first_gate) * (slot_gate(hot1) - slot_gate(hot2))
+    signed[...] = (logit_sent * n_sign).astype(BF16)
+    w_sign = jnp.where(hot1, logit_sent, 0.0) - jnp.where(hot2, logit_sent, 0.0)
+    wide[...] = weighted.astype(BF16)
+    wide_t[...] = weighted.T.astype(BF16)
+    scaled_t[...] = (gates * lows).T.astype(BF16)
+    sign_t[...] = w_sign.T.astype(BF16)
+
+    def partials(cc):
+        lines = pl.ds(pl.multiple_of(cc * 128, 128), 128)
+        slots = pl.ds(cc * 8, 8)
+
+        def dn_tile(i):
+            start = pl.multiple_of(i * TILE, TILE)
+            tile = jnp.dot(wide_t[lines, :], tok[:, pl.ds(start, TILE)], preferred_element_type=F32)
+            part[slots, :, pl.ds(start, TILE)] = tile.astype(BF16).reshape(8, 16, TILE)
+
+        def up_tile(i):
+            start = pl.multiple_of(i * TILE, TILE)
+            tile = jnp.dot(scaled_t[lines, :], gup[:, pl.ds(start, TILE)], preferred_element_type=F32)
+            part[slots, :, pl.ds(pl.multiple_of(model + start, TILE), TILE)] = tile.astype(
+                BF16
+            ).reshape(8, 16, TILE)
+
+        acc[...] = jnp.zeros_like(acc)
+        line = lax.broadcasted_iota(jnp.int32, (128, PIECE), 0) % 16
+
+        def router_tile(i):
+            cols = pl.ds(pl.multiple_of(i * PIECE, PIECE), PIECE)
+            tile = jnp.dot(sign_t[lines, :], tok[:, cols], preferred_element_type=F32)
+            acc[...] = jnp.where(line == i, tile, acc[...])
+
+        loop(model // TILE, dn_tile)
+        loop(hidden // TILE, up_tile)
+        loop(16, router_tile)
+        part[slots, :, pl.ds(both, PIECE)] = acc[...].astype(BF16).reshape(8, 16, PIECE)
+
+    def order(k):
+        low_half = (3, 2, 1 - z, z)[k]
+        high_half = (0, 1, 5 - z, z)[k]
+        return jnp.where(z < 2, low_half, high_half)
+
+    def core_copy(zz, xx):
+        at = zz * 2 + xx
+        return remote(
+            part.at[slot(1 - c, zz, xx)], core_in.at[at], core_send.at[at], core_recv.at[at], c_peer
+        )
+
+    def x_copy(zz):
+        return remote(
+            part.at[slot(c, zz, 1 - x)], x_in.at[zz], x_send.at[zz], x_recv.at[zz], x_peer
+        )
+
+    def right_copy(zz):
+        return remote(
+            part.at[slot(c, zz, x)], left_in.at[zz], z_send.at[zz], left_recv.at[zz], right
+        )
+
+    def left_copy(zz):
+        return remote(
+            part.at[slot(c, zz, x)], right_in.at[zz], z_send.at[zz], right_recv.at[zz], left
+        )
+
+    width = total // 7
+
+    def add(at, buf, index):
+        def tile(i):
+            cols = pl.ds(pl.multiple_of(i * width, 128), width)
+            part[at, :, cols] = (
+                part[at, :, cols].astype(F32) + buf[index, :, cols].astype(F32)
+            ).astype(BF16)
+
+        loop(7, tile)
+
+    partials(1 - c)
+    for k in range(4):
+        core_copy(order(k), 1 - x).start()
+    for k in range(4):
+        core_copy(order(k), x).start()
+    partials(c)
+    for k in range(4):
+        d = order(k)
+        core_copy(d, 1 - x).wait_recv()
+        add(slot(c, d, 1 - x), core_in, d * 2 + 1 - x)
+        x_copy(d).start()
+    for k in range(4):
+        d = order(k)
+        core_copy(d, x).wait_recv()
+        add(slot(c, d, x), core_in, d * 2 + x)
+
+    def token_tile(i):
+        start = pl.multiple_of(i * TILE, TILE)
+        cols = pl.ds(start, TILE)
+        tok_out[:, cols] = (
+            jnp.dot(wide[...], factor_tile(start), preferred_element_type=F32)
+            + jnp.dot(signed[...], router[:, cols], preferred_element_type=F32)
+        ).astype(BF16)
+
+    loop(model // TILE, token_tile)
+
+    for k in range(3):
+        d = order(k)
+        mine = slot(c, d, x)
+        x_copy(d).wait_recv()
+        add(mine, x_in, d)
+
+        def rightward(d=d, mine=mine):
+            def more():
+                right_copy(d).wait_recv()
+                add(mine, left_in, d)
+
+            pl.when(z > 0)(more)
+            right_copy(d).start()
+
+        def leftward(d=d, mine=mine):
+            def more():
+                left_copy(d).wait_recv()
+                add(mine, right_in, d)
+
+            pl.when(z < 3)(more)
+            left_copy(d).start()
+
+        pl.when(d > z)(rightward)
+        pl.when(d < z)(leftward)
+
+    def results(body):
+        def dn_tile(i):
+            start = pl.multiple_of(i * TILE, TILE)
+            body(dn_out, pl.ds(start, TILE), pl.ds(start, TILE))
+
+        def up_tile(i):
+            start = pl.multiple_of(i * TILE, TILE)
+            body(up_out, pl.ds(start, TILE), pl.ds(pl.multiple_of(model + start, TILE), TILE))
+
+        loop(model // TILE, dn_tile)
+        loop(hidden // TILE, up_tile)
+        body(rt_out, pl.ds(0, PIECE), pl.ds(both, PIECE))
+
+    def first_terms(out, here, there):
+        out[:, here] = part[own, :, there].astype(F32) + x_in[z, :, there].astype(F32)
+
+    def left_term(out, here, there):
+        out[:, here] += left_in[z, :, there].astype(F32)
+
+    def right_term(out, here, there):
+        out[:, here] += right_in[z, :, there].astype(F32)
+
+    def take_left():
+        right_copy(z).wait_recv()
+        results(left_term)
+
+    def take_right():
+        left_copy(z).wait_recv()
+        results(right_term)
+
+    x_copy(z).wait_recv()
+    results(first_terms)
+    pl.when(z > 0)(take_left)
+    pl.when(z < 3)(take_right)
+
+    for zz in range(4):
+        pl.when((z < 3) & (zz <= z))(lambda zz=zz: to_right(zz).wait_send())
+        pl.when((z > 0) & (zz >= z))(lambda zz=zz: to_left(zz).wait_send())
+        to_x(zz).wait_send()
+        x_copy(zz).wait_send()
+        pl.when(zz > z)(lambda zz=zz: right_copy(zz).wait_send())
+        pl.when(zz < z)(lambda zz=zz: left_copy(zz).wait_send())
+        for xx in range(2):
+            to_core(zz, xx).wait_send()
+            core_copy(zz, xx).wait_send()
+
+
+def fused(tokens, grad_up, tenant_ids, expert_ids, adapter_down, adapter_up, router):
+    rows, model = tokens.shape
+    hidden = grad_up.shape[1]
+    rank = adapter_down.shape[1]
+    both = model + hidden
+    total = both + PIECE
+    ids = tenant_ids[:, None] * EXP_TEN + expert_ids
+    vmem = pl.BlockSpec(memory_space=pltpu.VMEM)
+    dma = pltpu.SemaphoreType.DMA
+    tok_out, dn_out, up_out, rt_out = pl.pallas_call(
+        fused_kernel,
+        out_shape=(
+            jax.ShapeDtypeStruct((rows, model), BF16),
+            jax.ShapeDtypeStruct((rank, model), F32),
+            jax.ShapeDtypeStruct((rank, hidden), F32),
+            jax.ShapeDtypeStruct((16, PIECE), F32),
+        ),
+        in_specs=[vmem] * 6,
+        out_specs=(vmem,) * 4,
+        scratch_shapes=[
+            pltpu.VMEM((16, rank, both), BF16),
+            pltpu.VMEM((16, rank, total), BF16),
+            pltpu.VMEM((8, rank, total), BF16),
+            pltpu.VMEM((4, rank, total), BF16),
+            pltpu.VMEM((4, rank, total), BF16),
+            pltpu.VMEM((4, rank, total), BF16),
+            pltpu.VMEM((rows, 256), F32),
+            pltpu.VMEM((rows, 256), F32),
+            pltpu.VMEM((rows, 16), F32),
+            pltpu.VMEM((rows, 256), BF16),
+            pltpu.VMEM((256, rows), BF16),
+            pltpu.VMEM((256, rows), BF16),
+            pltpu.VMEM((256, rows), BF16),
+            pltpu.VMEM((rows, 16), BF16),
+            pltpu.VMEM((128, PIECE), F32),
+            dma((2,)), dma((20,)), dma((16,)), dma((8,)), dma((8,)),
+            dma((4,)), dma((4,)), dma((4,)), dma((4,)), dma((4,)),
+        ],
+        compiler_params=pltpu.CompilerParams(
+            collective_id=0, has_side_effects=True, vmem_limit_bytes=60 * 1024 * 1024
+        ),
+    )(tokens, grad_up, ids, adapter_down[0], adapter_up[0], router)
+    return (tok_out, dn_out[None], up_out[None], rt_out.reshape(1, model))
+
+
+def per_device(tokens, grad_up, tenant_ids, expert_ids, adapter_down, adapter_up, router):
+    fits = lax.axis_size("tenant") == 16 and tokens.shape[0] == 128 and adapter_down.shape[1] == 16
+    plan = fused if fits else routed
+    return plan(tokens, grad_up, tenant_ids, expert_ids, adapter_down, adapter_up, router)
+
+
 def solution(mesh):
     in_specs = (
         P(("group", "tenant"), None),

time: 550 us -> 186 us (0.34); the launches traced: 542 us -> 184 us
  waiting for transfers between devices: 351 us -> 0 us
  Pallas kernels: 0 us -> 175 us
  starting transfers between devices: 69.2 us -> 0 us
  local copies, waits for them, and re-layouts: 68.6 us -> 7.17 us
  matrix products: 27.2 us -> 0 us
  between operations: 14.7 us -> 0.64 us
  blocking collectives: 8.97 us -> 0 us
    all_to_all x4 -> x0, waiting for transfers between devices: 211 us -> none  [the longest x1 137 us: per_device(): lax.all_to_all(send_grads, 'tenant', split_axis=0, concat_axis=0, tiled=T...]
    pallas_call x0 -> x1, Pallas kernels: none -> 175 us  [fused(): pl.pallas_call(fused_kernel, out_shape=(jax.ShapeDtypeStruct((rows, model...]
    unnamed x2 -> x0, waiting for transfers between devices: 140 us -> none
    all_to_all x4 -> x0, starting transfers between devices: 68.9 us -> none  [the longest x1 36.9 us: per_device(): lax.all_to_all(send_rows, 'tenant', split_axis=0, concat_axis=0, tiled=True)]
    scatter x6 -> x0, local copies, waits for them, and re-layouts: 45.1 us -> none  [the longest x4 42.4 us: spread_rows(): return empty.at[places[:, 0]].set(values).at[places[:, 1]].set(values)]
    dot_general x8 -> x0, matrix products: 27.2 us -> none  [the longest x1 5.68 us: per_device(): lax.dot_general(grads_in, upper, (((1,), (1,)), ((), ())), preferred_elem...]
    gather x8 -> x0, local copies, waits for them, and re-layouts: 18.6 us -> none  [the longest x1 7.81 us: per_device(): flat_back[places[:, 1]].astype(jnp.float32)]
    all_to_all x1 -> x0, blocking collectives: 8.97 us -> none  [per_device(): lax.all_to_all(send_gates, 'tenant', split_axis=0, concat_axis=0, tiled=T...]
  transfers between devices with their start and end apart: 5 -> 0, of which waited for: 4 -> 0; matrix products, arithmetic and copies ran while one was open for 7% -> 0% of each run, Pallas kernels for 0% -> 0%
where the time goes in v2:
time: 186 us; the launch traced here: 184 us
  Pallas kernels  175 us (94%)
  local copies, waits for them, and re-layouts  7.17 us (4%)
    pallas_call x1, Pallas kernels, fused(): pl.pallas_call(fused_kernel, out_shape=(jax.ShapeDtypeStruct((rows, model...  175 us
    unnamed x9, local copies, waits for them, and re-layouts  7.17 us

profile of v2, /device:TPU:0, one launch (start us, length us, event | category | flops | bytes accessed | tf_op | source)
XLA Modules:
  0.0 184.1 jit_solution(11162984889652826991)
XLA Ops:
  0.6 0.7 broadcast_multiply_fusion
  1.3 0.8 copy.13
  2.1 0.7 broadcast_add_fusion.ids
  2.8 174.9 %shard_map.102 = (bf16[128,8192]{1,0:T(8,128)(2,1)}, f32[16,8192]{1,0:T(8,128)}, f32[16,16384]{1,0:T(8,128)}, f32[16,512]{1,0:T(8,128)}) custom-call(bf16[128,8192]{1,0:T(8,128)(2,1)} %tok.1, bf16[128,16384]{1,0:T(8,128)(2,1)} %gup.1, s32[128,2]{1,0:T(8,128)} %broadcast_add_fusion.ids, bf16[16,8192]{1,0:T(8,128)(2,1)} %bitcast.10, ...), custom_call_target="tpu_custom_call" | custom-call | tf_op jit(solution)/shard_map/pallas_call | solution.py:482
  177.7 1.4 copy.14
  179.1 0.0 copy-start.1
  179.1 0.0 copy-start
  179.1 3.2 %copy.18 = bf16[128,8192]{1,0:T(8,128)(2,1)} copy(bf16[128,8192]{1,0:T(8,128)(2,1)} %get-tuple-element.16) | data formatting | bytes 4194304
  182.3 0.0 copy-done.1
  182.3 0.8 copy.19
  183.1 0.0 copy-done
  183.1 1.0 copy.20
Async XLA Ops:
  179.1 3.2 %copy-start.1 = (f32[16,8192]{1,0:T(8,128)S(1)}, f32[16,8192]{1,0:T(8,128)}, u32[]{:S(2)}) copy-start(f32[16,8192]{1,0:T(8,128)} %get-tuple-element.9) | copy-start | bytes 1572868
  179.1 4.0 %copy-start = (f32[16,16384]{1,0:T(8,128)S(1)}, f32[16,16384]{1,0:T(8,128)}, u32[]{:S(2)}) copy-start(f32[16,16384]{1,0:T(8,128)} %get-tuple-element.10) | copy-start | bytes 3145732

commit v3 on v2

--- a/solution.py
+++ b/solution.py
@@ -146,14 +146,16 @@
     tok_out, dn_out, up_out, rt_out,
     fac, part, core_in, x_in, left_in, right_in,
     low, back, logits, wide, wide_t, scaled_t, sign_t, signed, acc,
-    own_sem, ag_send, ag_recv, core_send, core_recv, x_send, x_recv, z_send, left_recv, right_recv,
+    own_sem, ag_send, ag_recv, y_send, y_recv, core_send, core_recv, x_send, x_recv, z_send, left_recv, right_recv,
 ):
     me = lax.axis_index("tenant")
+    g = lax.axis_index("group")
     c = lax.rem(me, 2)
     x = lax.rem(lax.div(me, 2), 2)
     z = lax.div(me, 4)
     model = tok.shape[1]
     hidden = gup.shape[1]
+    half = hidden // 2
     both = model + hidden
     total = part.shape[2]
     rows = tok.shape[0]
@@ -168,34 +170,64 @@
 
     barrier = pltpu.get_barrier_semaphore()
 
-    def greet(peer):
+    def greet(peer, group=g):
         pl.semaphore_signal(
-            barrier, inc=1, device_id={"tenant": peer}, device_id_type=pl.DeviceIdType.MESH
+            barrier,
+            inc=1,
+            device_id={"group": group, "tenant": peer},
+            device_id_type=pl.DeviceIdType.MESH,
         )
 
     own = slot(c, z, x)
-    own_dn = pltpu.make_async_copy(adn, fac.at[own, :, pl.ds(0, model)], own_sem.at[0])
-    own_up = pltpu.make_async_copy(aup, fac.at[own, :, pl.ds(model, hidden)], own_sem.at[1])
+    own_dn = pltpu.make_async_copy(adn, fac.at[own, :, pl.ds(half, model)], own_sem.at[0])
+    own_lo = pltpu.make_async_copy(
+        aup.at[:, pl.ds(0, half)], fac.at[own, :, pl.ds(0, half)], own_sem.at[1]
+    )
+    own_hi = pltpu.make_async_copy(
+        aup.at[:, pl.ds(half, half)], fac.at[own, :, pl.ds(half + model, half)], own_sem.at[2]
+    )
     own_dn.start()
-    own_up.start()
+    own_lo.start()
+    own_hi.start()
     greet(x_peer)
     greet(c_peer)
+    greet(me, 1 - g)
     pl.when(z < 3)(lambda: greet(right))
     pl.when(z > 0)(lambda: greet(left))
     pl.semaphore_wait(
-        barrier, 2 + jnp.where(z < 3, 1, 0).astype(jnp.int32) + jnp.where(z > 0, 1, 0).astype(jnp.int32)
+        barrier, 3 + jnp.where(z < 3, 1, 0).astype(jnp.int32) + jnp.where(z > 0, 1, 0).astype(jnp.int32)
     )
     own_dn.wait()
-    own_up.wait()
-
-    def remote(src, dst, send, recv, peer):
+    own_lo.wait()
+    own_hi.wait()
+
+    def remote(src, dst, send, recv, peer, group=g):
         return pltpu.make_async_remote_copy(
             src_ref=src, dst_ref=dst, send_sem=send, recv_sem=recv,
-            device_id={"tenant": peer}, device_id_type=pl.DeviceIdType.MESH,
-        )
+            device_id={"group": group, "tenant": peer}, device_id_type=pl.DeviceIdType.MESH,
+        )
+
+    gathered = pl.ds(pl.multiple_of(g * half, 128), half + model)
+    mine_y = pl.ds(pl.multiple_of(g * (half + model), 128), half)
+    other_y = pl.ds(pl.multiple_of((1 - g) * (half + model), 128), half)
 
     def gather_copy(at, send_at, peer):
-        return remote(fac.at[at], fac.at[at], ag_send.at[send_at], ag_recv.at[at], peer)
+        block = fac.at[at, :, gathered]
+        return remote(block, block, ag_send.at[send_at], ag_recv.at[at], peer)
+
+    def to_y(zz, xx):
+        at = slot(c, zz, xx)
+        block = fac.at[at, :, mine_y]
+        return remote(block, block, y_send.at[zz * 2 + xx], y_recv.at[at], me, 1 - g)
+
+    def y_to_core(zz, xx):
+        at = slot(c, zz, xx)
+        block = fac.at[at, :, other_y]
+        return remote(block, block, y_send.at[8 + zz * 2 + xx], y_recv.at[at], c_peer)
+
+    def y_arrived(at):
+        block = fac.at[at, :, other_y]
+        remote(block, block, y_send.at[0], y_recv.at[at], c_peer).wait_recv()
 
     def to_right(zz):
         return gather_copy(slot(c, zz, x), zz, right)
@@ -216,6 +248,7 @@
     pl.when(z > 0)(lambda: to_left(z).start())
     to_x(z).start()
     to_core(z, x).start()
+    y_to_core(z, x).start()
 
     nt = (((1,), (1,)), ((), ()))
     logits[...] = jnp.zeros_like(logits)
@@ -231,12 +264,14 @@
             arrived(slot(c, z - s, x))
             pl.when(z < 3)(lambda: to_right(z - s).start())
             to_x(z - s).start()
+            to_y(z - s, x).start()
             to_core(z - s, x).start()
 
         def from_right(s=s):
             arrived(slot(c, z + s, x))
             pl.when(z > 0)(lambda: to_left(z + s).start())
             to_x(z + s).start()
+            to_y(z + s, x).start()
             to_core(z + s, x).start()
 
         pl.when(z - s >= 0)(from_left)
@@ -244,12 +279,22 @@
 
     def x_block(zz):
         arrived(slot(c, zz, 1 - x))
+        to_y(zz, 1 - x).start()
         to_core(zz, 1 - x).start()
+
+    def y_block(zz, xx):
+        y_arrived(slot(c, zz, xx))
+        y_to_core(zz, xx).start()
 
     x_block(z)
     for s in range(1, 4):
-        pl.when(z - s >= 0)(functools.partial(x_block, z - s))
-        pl.when(z + s <= 3)(functools.partial(x_block, z + s))
+        for inside, zz in ((z - s >= 0, z - s), (z + s <= 3, z + s)):
+            pl.when(inside)(functools.partial(y_block, zz, x))
+            pl.when(inside)(functools.partial(x_block, zz))
+    y_block(z, 1 - x)
+    for s in range(1, 4):
+        for inside, zz in ((z - s >= 0, z - s), (z + s <= 3, z + s)):
+            pl.when(inside)(functools.partial(y_block, zz, 1 - x))
     for k in range(8):
         arrived((1 - c) * 8 + k)
 
@@ -262,19 +307,24 @@
     def low_tile(i):
         start = pl.multiple_of(i * TILE, TILE)
         low[...] += lax.dot_general(
-            tok[:, pl.ds(start, TILE)], factor_tile(start), nt, preferred_element_type=F32
+            tok[:, pl.ds(start, TILE)],
+            factor_tile(pl.multiple_of(half + start, TILE)),
+            nt,
+            preferred_element_type=F32
         )
 
     def back_tile(i):
         start = pl.multiple_of(i * TILE, TILE)
         back[...] += lax.dot_general(
             gup[:, pl.ds(start, TILE)],
-            factor_tile(pl.multiple_of(model + start, TILE)),
+            factor_tile(pl.multiple_of(start + jnp.where(start >= half, model, 0), TILE)),
             nt,
             preferred_element_type=F32,
         )
 
     loop(model // TILE, low_tile)
+    for k in range(8):
+        y_arrived((1 - c) * 8 + k)
     loop(hidden // TILE, back_tile)
 
     first = ids[:, 0:1]
@@ -392,7 +442,9 @@
         start = pl.multiple_of(i * TILE, TILE)
         cols = pl.ds(start, TILE)
         tok_out[:, cols] = (
-            jnp.dot(wide[...], factor_tile(start), preferred_element_type=F32)
+            jnp.dot(
+                wide[...], factor_tile(pl.multiple_of(half + start, TILE)), preferred_element_type=F32
+            )
             + jnp.dot(signed[...], router[:, cols], preferred_element_type=F32)
         ).astype(BF16)
 
@@ -467,6 +519,8 @@
         pl.when(zz < z)(lambda zz=zz: left_copy(zz).wait_send())
         for xx in range(2):
             to_core(zz, xx).wait_send()
+            y_to_core(zz, xx).wait_send()
+            pl.when((zz != z) | (xx != x))(lambda zz=zz, xx=xx: to_y(zz, xx).wait_send())
             core_copy(zz, xx).wait_send()
 
 
@@ -505,7 +559,7 @@
             pltpu.VMEM((256, rows), BF16),
             pltpu.VMEM((rows, 16), BF16),
             pltpu.VMEM((128, PIECE), F32),
-            dma((2,)), dma((20,)), dma((16,)), dma((8,)), dma((8,)),
+            dma((3,)), dma((20,)), dma((16,)), dma((16,)), dma((16,)), dma((8,)), dma((8,)),
             dma((4,)), dma((4,)), dma((4,)), dma((4,)), dma((4,)),
         ],
         compiler_params=pltpu.CompilerParams(
@@ -516,7 +570,8 @@
 
 
 def per_device(tokens, grad_up, tenant_ids, expert_ids, adapter_down, adapter_up, router):
-    fits = lax.axis_size("tenant") == 16 and tokens.shape[0] == 128 and adapter_down.shape[1] == 16
+    planes = lax.axis_size("tenant") == 16 and lax.axis_size("group") == 2
+    fits = planes and tokens.shape[0] == 128 and adapter_down.shape[1] == 16
     plan = fused if fits else routed
     return plan(tokens, grad_up, tenant_ids, expert_ids, adapter_down, adapter_up, router)
 

time: 186 us -> 180 us (0.968); the launches traced: 184 us -> 180 us
  Pallas kernels: 175 us -> 171 us
    pallas_call x1, Pallas kernels: 175 us -> 171 us  [fused(): pl.pallas_call(fused_kernel, out_shape=(jax.ShapeDtypeStruct((rows, model...]
where the time goes in v3:
time: 180 us
  Pallas kernels  171 us (95%)
  local copies, waits for them, and re-layouts  7.17 us (4%)
    pallas_call x1, Pallas kernels, fused(): pl.pallas_call(fused_kernel, out_shape=(jax.ShapeDtypeStruct((rows, model...  171 us
    unnamed x9, local copies, waits for them, and re-layouts  7.17 us

profile of v3, /device:TPU:0, one launch (start us, length us, event | category | flops | bytes accessed | tf_op | source)
XLA Modules:
  0.0 180.1 jit_solution(3206450475428730443)
XLA Ops:
  0.6 0.7 broadcast_multiply_fusion
  1.3 0.8 copy.13
  2.1 0.7 broadcast_add_fusion.ids
  2.8 171.0 %shard_map.102 = (bf16[128,8192]{1,0:T(8,128)(2,1)}, f32[16,8192]{1,0:T(8,128)}, f32[16,16384]{1,0:T(8,128)}, f32[16,512]{1,0:T(8,128)}) custom-call(bf16[128,8192]{1,0:T(8,128)(2,1)} %tok.1, bf16[128,16384]{1,0:T(8,128)(2,1)} %gup.1, s32[128,2]{1,0:T(8,128)} %broadcast_add_fusion.ids, bf16[16,8192]{1,0:T(8,128)(2,1)} %bitcast.10, ...), custom_call_target="tpu_custom_call" | custom-call | tf_op jit(solution)/shard_map/pallas_call | solution.py:536
  173.8 1.4 copy.14
  175.2 0.0 copy-start.1
  175.2 0.0 copy-start
  175.2 3.2 %copy.18 = bf16[128,8192]{1,0:T(8,128)(2,1)} copy(bf16[128,8192]{1,0:T(8,128)(2,1)} %get-tuple-element.16) | data formatting | bytes 4194304
  178.4 0.0 copy-done.1
  178.4 0.8 copy.19
  179.2 0.0 copy-done
  179.2 1.0 copy.20
Async XLA Ops:
  175.2 3.2 %copy-start.1 = (f32[16,8192]{1,0:T(8,128)S(1)}, f32[16,8192]{1,0:T(8,128)}, u32[]{:S(2)}) copy-start(f32[16,8192]{1,0:T(8,128)} %get-tuple-element.9) | copy-start | bytes 1572868
  175.2 4.0 %copy-start = (f32[16,16384]{1,0:T(8,128)S(1)}, f32[16,16384]{1,0:T(8,128)}, u32[]{:S(2)}) copy-start(f32[16,16384]{1,0:T(8,128)} %get-tuple-element.10) | copy-start | bytes 3145732

commit v4 on v3

--- a/solution.py
+++ b/solution.py
@@ -356,87 +356,107 @@
     scaled_t[...] = (gates * lows).T.astype(BF16)
     sign_t[...] = w_sign.T.astype(BF16)
 
-    def partials(cc):
-        lines = pl.ds(pl.multiple_of(cc * 128, 128), 128)
-        slots = pl.ds(cc * 8, 8)
-
-        def dn_tile(i):
-            start = pl.multiple_of(i * TILE, TILE)
-            tile = jnp.dot(wide_t[lines, :], tok[:, pl.ds(start, TILE)], preferred_element_type=F32)
-            part[slots, :, pl.ds(start, TILE)] = tile.astype(BF16).reshape(8, 16, TILE)
-
-        def up_tile(i):
-            start = pl.multiple_of(i * TILE, TILE)
-            tile = jnp.dot(scaled_t[lines, :], gup[:, pl.ds(start, TILE)], preferred_element_type=F32)
-            part[slots, :, pl.ds(pl.multiple_of(model + start, TILE), TILE)] = tile.astype(
-                BF16
-            ).reshape(8, 16, TILE)
-
+    chunks = ((0, model), (model, half), (model + half, half + PIECE))
+
+    def dn_products():
+        def tile(i):
+            cols = pl.ds(pl.multiple_of(i * PIECE, PIECE), PIECE)
+            made = jnp.dot(wide_t[...], tok[:, cols], preferred_element_type=F32)
+            part[:, :, cols] = made.astype(BF16).reshape(16, 16, PIECE)
+
+        loop(model // PIECE, tile)
+
+    def up_products(start):
+        def tile(i):
+            at = pl.multiple_of(start + i * PIECE, PIECE)
+            made = jnp.dot(scaled_t[...], gup[:, pl.ds(at, PIECE)], preferred_element_type=F32)
+            part[:, :, pl.ds(pl.multiple_of(model + at, PIECE), PIECE)] = made.astype(BF16).reshape(
+                16, 16, PIECE
+            )
+
+        loop(half // PIECE, tile)
+
+    def router_products():
         acc[...] = jnp.zeros_like(acc)
-        line = lax.broadcasted_iota(jnp.int32, (128, PIECE), 0) % 16
-
-        def router_tile(i):
+        line = lax.broadcasted_iota(jnp.int32, (256, PIECE), 0) % 16
+
+        def tile(i):
             cols = pl.ds(pl.multiple_of(i * PIECE, PIECE), PIECE)
-            tile = jnp.dot(sign_t[lines, :], tok[:, cols], preferred_element_type=F32)
-            acc[...] = jnp.where(line == i, tile, acc[...])
-
-        loop(model // TILE, dn_tile)
-        loop(hidden // TILE, up_tile)
-        loop(16, router_tile)
-        part[slots, :, pl.ds(both, PIECE)] = acc[...].astype(BF16).reshape(8, 16, PIECE)
+            made = jnp.dot(sign_t[...], tok[:, cols], preferred_element_type=F32)
+            acc[...] = jnp.where(line == i, made, acc[...])
+
+        loop(16, tile)
+        part[:, :, pl.ds(both, PIECE)] = acc[...].astype(BF16).reshape(16, 16, PIECE)
 
     def order(k):
         low_half = (3, 2, 1 - z, z)[k]
         high_half = (0, 1, 5 - z, z)[k]
         return jnp.where(z < 2, low_half, high_half)
 
-    def core_copy(zz, xx):
+    def reduce_copy(q, source, target, to, send, recv, sem_at, peer):
+        cols = pl.ds(*chunks[q])
+        return remote(
+            part.at[source, :, cols], target.at[to, :, cols],
+            send.at[q, sem_at], recv.at[q, sem_at], peer,
+        )
+
+    def core_copy(q, zz, xx):
         at = zz * 2 + xx
-        return remote(
-            part.at[slot(1 - c, zz, xx)], core_in.at[at], core_send.at[at], core_recv.at[at], c_peer
+        return reduce_copy(
+            q, slot(1 - c, zz, xx), core_in, at, core_send, core_recv, at, c_peer
         )
 
-    def x_copy(zz):
-        return remote(
-            part.at[slot(c, zz, 1 - x)], x_in.at[zz], x_send.at[zz], x_recv.at[zz], x_peer
-        )
-
-    def right_copy(zz):
-        return remote(
-            part.at[slot(c, zz, x)], left_in.at[zz], z_send.at[zz], left_recv.at[zz], right
-        )
-
-    def left_copy(zz):
-        return remote(
-            part.at[slot(c, zz, x)], right_in.at[zz], z_send.at[zz], right_recv.at[zz], left
-        )
-
-    width = total // 7
-
-    def add(at, buf, index):
-        def tile(i):
-            cols = pl.ds(pl.multiple_of(i * width, 128), width)
+    def x_copy(q, zz):
+        return reduce_copy(q, slot(c, zz, 1 - x), x_in, zz, x_send, x_recv, zz, x_peer)
+
+    def right_copy(q, zz):
+        return reduce_copy(q, slot(c, zz, x), left_in, zz, z_send, left_recv, zz, right)
+
+    def left_copy(q, zz):
+        return reduce_copy(q, slot(c, zz, x), right_in, zz, z_send, right_recv, zz, left)
+
+    def add(q, at, buf, index):
+        begin, size = chunks[q]
+
+        def add_cols(cols):
             part[at, :, cols] = (
                 part[at, :, cols].astype(F32) + buf[index, :, cols].astype(F32)
             ).astype(BF16)
 
-        loop(7, tile)
-
-    partials(1 - c)
-    for k in range(4):
-        core_copy(order(k), 1 - x).start()
-    for k in range(4):
-        core_copy(order(k), x).start()
-    partials(c)
-    for k in range(4):
-        d = order(k)
-        core_copy(d, 1 - x).wait_recv()
-        add(slot(c, d, 1 - x), core_in, d * 2 + 1 - x)
-        x_copy(d).start()
-    for k in range(4):
-        d = order(k)
-        core_copy(d, x).wait_recv()
-        add(slot(c, d, x), core_in, d * 2 + x)
+        loop(size // 2048, lambda i: add_cols(pl.ds(pl.multiple_of(begin + i * 2048, PIECE), 2048)))
+        if size % 2048:
+            add_cols(pl.ds(begin + size // 2048 * 2048, size % 2048))
+
+    def to_core_peer(q):
+        for k in range(4):
+            core_copy(q, order(k), 1 - x).start()
+        for k in range(4):
+            core_copy(q, order(k), x).start()
+
+    def x_stage(q):
+        for k in range(4):
+            d = order(k)
+            core_copy(q, d, 1 - x).wait_recv()
+            add(q, slot(c, d, 1 - x), core_in, d * 2 + 1 - x)
+            x_copy(q, d).start()
+
+    def own_stage(q):
+        for k in range(4):
+            d = order(k)
+            core_copy(q, d, x).wait_recv()
+            add(q, slot(c, d, x), core_in, d * 2 + x)
+
+    dn_products()
+    to_core_peer(0)
+    up_products(0)
+    to_core_peer(1)
+    x_stage(0)
+    up_products(half)
+    router_products()
+    to_core_peer(2)
+    x_stage(1)
+    own_stage(0)
+    x_stage(2)
 
     def token_tile(i):
         start = pl.multiple_of(i * TILE, TILE)
@@ -448,32 +468,38 @@
             + jnp.dot(signed[...], router[:, cols], preferred_element_type=F32)
         ).astype(BF16)
 
+    def z_stage(q):
+        for k in range(3):
+            d = order(k)
+            mine = slot(c, d, x)
+            x_copy(q, d).wait_recv()
+            add(q, mine, x_in, d)
+
+            def rightward(d=d, mine=mine):
+                def more():
+                    right_copy(q, d).wait_recv()
+                    add(q, mine, left_in, d)
+
+                pl.when(z > 0)(more)
+                right_copy(q, d).start()
+
+            def leftward(d=d, mine=mine):
+                def more():
+                    left_copy(q, d).wait_recv()
+                    add(q, mine, right_in, d)
+
+                pl.when(z < 3)(more)
+                left_copy(q, d).start()
+
+            pl.when(d > z)(rightward)
+            pl.when(d < z)(leftward)
+
+    z_stage(0)
+    own_stage(1)
+    own_stage(2)
     loop(model // TILE, token_tile)
-
-    for k in range(3):
-        d = order(k)
-        mine = slot(c, d, x)
-        x_copy(d).wait_recv()
-        add(mine, x_in, d)
-
-        def rightward(d=d, mine=mine):
-            def more():
-                right_copy(d).wait_recv()
-                add(mine, left_in, d)
-
-            pl.when(z > 0)(more)
-            right_copy(d).start()
-
-        def leftward(d=d, mine=mine):
-            def more():
-                left_copy(d).wait_recv()
-                add(mine, right_in, d)
-
-            pl.when(z < 3)(more)
-            left_copy(d).start()
-
-        pl.when(d > z)(rightward)
-        pl.when(d < z)(leftward)
+    z_stage(1)
+    z_stage(2)
 
     def results(body):
         def dn_tile(i):
@@ -498,14 +524,17 @@
         out[:, here] += right_in[z, :, there].astype(F32)
 
     def take_left():
-        right_copy(z).wait_recv()
+        for q in range(3):
+            right_copy(q, z).wait_recv()
         results(left_term)
 
     def take_right():
-        left_copy(z).wait_recv()
+        for q in range(3):
+            left_copy(q, z).wait_recv()
         results(right_term)
 
-    x_copy(z).wait_recv()
+    for q in range(3):
+        x_copy(q, z).wait_recv()
     results(first_terms)
     pl.when(z > 0)(take_left)
     pl.when(z < 3)(take_right)
@@ -514,14 +543,16 @@
         pl.when((z < 3) & (zz <= z))(lambda zz=zz: to_right(zz).wait_send())
         pl.when((z > 0) & (zz >= z))(lambda zz=zz: to_left(zz).wait_send())
         to_x(zz).wait_send()
-        x_copy(zz).wait_send()
-        pl.when(zz > z)(lambda zz=zz: right_copy(zz).wait_send())
-        pl.when(zz < z)(lambda zz=zz: left_copy(zz).wait_send())
+        for q in range(3):
+            x_copy(q, zz).wait_send()
+            pl.when(zz > z)(lambda q=q, zz=zz: right_copy(q, zz).wait_send())
+            pl.when(zz < z)(lambda q=q, zz=zz: left_copy(q, zz).wait_send())
         for xx in range(2):
             to_core(zz, xx).wait_send()
             y_to_core(zz, xx).wait_send()
             pl.when((zz != z) | (xx != x))(lambda zz=zz, xx=xx: to_y(zz, xx).wait_send())
-            core_copy(zz, xx).wait_send()
+            for q in range(3):
+                core_copy(q, zz, xx).wait_send()
 
 
 def fused(tokens, grad_up, tenant_ids, expert_ids, adapter_down, adapter_up, router):
@@ -558,9 +589,9 @@
             pltpu.VMEM((256, rows), BF16),
             pltpu.VMEM((256, rows), BF16),
             pltpu.VMEM((rows, 16), BF16),
-            pltpu.VMEM((128, PIECE), F32),
-            dma((3,)), dma((20,)), dma((16,)), dma((16,)), dma((16,)), dma((8,)), dma((8,)),
-            dma((4,)), dma((4,)), dma((4,)), dma((4,)), dma((4,)),
+            pltpu.VMEM((256, PIECE), F32),
+            dma((3,)), dma((20,)), dma((16,)), dma((16,)), dma((16,)), dma((3, 8)), dma((3, 8)),
+            dma((3, 4)), dma((3, 4)), dma((3, 4)), dma((3, 4)), dma((3, 4)),
         ],
         compiler_params=pltpu.CompilerParams(
             collective_id=0, has_side_effects=True, vmem_limit_bytes=60 * 1024 * 1024

time: 180 us -> 174 us (0.967)
  Pallas kernels: 171 us -> 164 us
    pallas_call x1, Pallas kernels: 171 us -> 164 us  [fused(): pl.pallas_call(fused_kernel, out_shape=(jax.ShapeDtypeStruct((rows, model...]
where the time goes in v4:
time: 174 us; the launch traced here: 173 us
  Pallas kernels  164 us (94%)
  local copies, waits for them, and re-layouts  7.17 us (4%)
    pallas_call x1, Pallas kernels, fused(): pl.pallas_call(fused_kernel, out_shape=(jax.ShapeDtypeStruct((rows, model...  164 us
    unnamed x9, local copies, waits for them, and re-layouts  7.17 us

profile of v4, /device:TPU:0, one launch (start us, length us, event | category | flops | bytes accessed | tf_op | source)
XLA Modules:
  0.0 173.4 jit_solution(7607921109726338107)
XLA Ops:
  0.6 0.7 broadcast_multiply_fusion
  1.3 0.8 copy.13
  2.1 0.7 broadcast_add_fusion.ids
  2.8 164.2 %shard_map.102 = (bf16[128,8192]{1,0:T(8,128)(2,1)}, f32[16,8192]{1,0:T(8,128)}, f32[16,16384]{1,0:T(8,128)}, f32[16,512]{1,0:T(8,128)}) custom-call(bf16[128,8192]{1,0:T(8,128)(2,1)} %tok.1, bf16[128,16384]{1,0:T(8,128)(2,1)} %gup.1, s32[128,2]{1,0:T(8,128)} %broadcast_add_fusion.ids, bf16[16,8192]{1,0:T(8,128)(2,1)} %bitcast.10, ...), custom_call_target="tpu_custom_call" | custom-call | tf_op jit(solution)/shard_map/pallas_call | solution.py:567
  167.0 1.4 copy.14
  168.4 0.0 copy-start.1
  168.4 0.0 copy-start
  168.4 3.2 %copy.18 = bf16[128,8192]{1,0:T(8,128)(2,1)} copy(bf16[128,8192]{1,0:T(8,128)(2,1)} %get-tuple-element.16) | data formatting | bytes 4194304
  171.6 0.0 copy-done.1
  171.6 0.8 copy.19
  172.4 0.0 copy-done
  172.4 1.0 copy.20
Async XLA Ops:
  168.4 3.2 %copy-start.1 = (f32[16,8192]{1,0:T(8,128)S(1)}, f32[16,8192]{1,0:T(8,128)}, u32[]{:S(2)}) copy-start(f32[16,8192]{1,0:T(8,128)} %get-tuple-element.9) | copy-start | bytes 1572868
  168.4 4.0 %copy-start = (f32[16,16384]{1,0:T(8,128)S(1)}, f32[16,16384]{1,0:T(8,128)}, u32[]{:S(2)}) copy-start(f32[16,16384]{1,0:T(8,128)} %get-tuple-element.10) | copy-start | bytes 3145732

commit v5 on v4

--- a/solution.py
+++ b/solution.py
@@ -142,9 +142,9 @@
 
 
 def fused_kernel(
-    tok, gup, ids, adn, aup, router,
+    tok_in, gup_in, ids, adn, aup, router,
     tok_out, dn_out, up_out, rt_out,
-    fac, part, core_in, x_in, left_in, right_in,
+    tok, gup, fac, part, core_in, x_in, left_in, right_in,
     low, back, logits, wide, wide_t, scaled_t, sign_t, signed, acc,
     own_sem, ag_send, ag_recv, y_send, y_recv, core_send, core_recv, x_send, x_recv, z_send, left_recv, right_recv,
 ):
@@ -189,6 +189,10 @@
     own_dn.start()
     own_lo.start()
     own_hi.start()
+    load_tok = pltpu.make_async_copy(tok_in, tok, own_sem.at[3])
+    load_gup = pltpu.make_async_copy(gup_in, gup, own_sem.at[4])
+    load_tok.start()
+    load_gup.start()
     greet(x_peer)
     greet(c_peer)
     greet(me, 1 - g)
@@ -257,6 +261,7 @@
         cols = pl.ds(pl.multiple_of(i * TILE, TILE), TILE)
         logits[...] += lax.dot_general(tok[:, cols], router[:, cols], nt, preferred_element_type=F32)
 
+    load_tok.wait()
     loop(model // TILE, logit_tile)
 
     for s in range(1, 4):
@@ -323,9 +328,12 @@
         )
 
     loop(model // TILE, low_tile)
+    load_gup.wait()
+    per_half = half // TILE
+    loop(per_half, lambda i: back_tile(i + g * per_half))
     for k in range(8):
         y_arrived((1 - c) * 8 + k)
-    loop(hidden // TILE, back_tile)
+    loop(per_half, lambda i: back_tile(i + (1 - g) * per_half))
 
     first = ids[:, 0:1]
     second = ids[:, 1:2]
@@ -563,6 +571,7 @@
     total = both + PIECE
     ids = tenant_ids[:, None] * EXP_TEN + expert_ids
     vmem = pl.BlockSpec(memory_space=pltpu.VMEM)
+    hbm = pl.BlockSpec(memory_space=pl.ANY)
     dma = pltpu.SemaphoreType.DMA
     tok_out, dn_out, up_out, rt_out = pl.pallas_call(
         fused_kernel,
@@ -572,9 +581,11 @@
             jax.ShapeDtypeStruct((rank, hidden), F32),
             jax.ShapeDtypeStruct((16, PIECE), F32),
         ),
-        in_specs=[vmem] * 6,
+        in_specs=[hbm, hbm, vmem, hbm, hbm, vmem],
         out_specs=(vmem,) * 4,
         scratch_shapes=[
+            pltpu.VMEM((rows, model), BF16),
+            pltpu.VMEM((rows, hidden), BF16),
             pltpu.VMEM((16, rank, both), BF16),
             pltpu.VMEM((16, rank, total), BF16),
             pltpu.VMEM((8, rank, total), BF16),
@@ -590,7 +601,7 @@
             pltpu.VMEM((256, rows), BF16),
             pltpu.VMEM((rows, 16), BF16),
             pltpu.VMEM((256, PIECE), F32),
-            dma((3,)), dma((20,)), dma((16,)), dma((16,)), dma((16,)), dma((3, 8)), dma((3, 8)),
+            dma((5,)), dma((20,)), dma((16,)), dma((16,)), dma((16,)), dma((3, 8)), dma((3, 8)),
             dma((3, 4)), dma((3, 4)), dma((3, 4)), dma((3, 4)), dma((3, 4)),
         ],
         compiler_params=pltpu.CompilerParams(

time: 174 us -> 173 us (level)
  no operation moved by 1% of the time
where the time goes in v5:
time: 173 us
  Pallas kernels  164 us (95%)
  local copies, waits for them, and re-layouts  7.17 us (4%)
    pallas_call x1, Pallas kernels, fused(): pl.pallas_call(fused_kernel, out_shape=(jax.ShapeDtypeStruct((rows, model...  164 us
    unnamed x9, local copies, waits for them, and re-layouts  7.17 us

profile of v5, /device:TPU:0, one launch (start us, length us, event | category | flops | bytes accessed | tf_op | source)
XLA Modules:
  0.0 173.0 jit_solution(10666391835141689256)
XLA Ops:
  0.6 0.7 broadcast_multiply_fusion
  1.3 0.8 copy.13
  2.1 0.7 broadcast_add_fusion.ids
  2.8 163.8 %shard_map.102 = (bf16[128,8192]{1,0:T(8,128)(2,1)}, f32[16,8192]{1,0:T(8,128)}, f32[16,16384]{1,0:T(8,128)}, f32[16,512]{1,0:T(8,128)}) custom-call(bf16[128,8192]{1,0:T(8,128)(2,1)} %tok_in.1, bf16[128,16384]{1,0:T(8,128)(2,1)} %gup_in.1, s32[128,2]{1,0:T(8,128)} %broadcast_add_fusion.ids, bf16[16,8192]{1,0:T(8,128)(2,1)} %bitcast.10, ...), custom_call_target="tpu_custom_call" | custom-call | tf_op jit(solution)/shard_map/pallas_call | solution.py:576
  166.6 1.4 copy.14
  168.0 0.0 copy-start.1
  168.0 0.0 copy-start
  168.0 3.2 %copy.18 = bf16[128,8192]{1,0:T(8,128)(2,1)} copy(bf16[128,8192]{1,0:T(8,128)(2,1)} %get-tuple-element.16) | data formatting | bytes 4194304
  171.2 0.0 copy-done.1
  171.2 0.8 copy.19
  172.0 0.0 copy-done
  172.0 1.0 copy.20
Async XLA Ops:
  168.0 3.2 %copy-start.1 = (f32[16,8192]{1,0:T(8,128)S(1)}, f32[16,8192]{1,0:T(8,128)}, u32[]{:S(2)}) copy-start(f32[16,8192]{1,0:T(8,128)} %get-tuple-element.9) | copy-start | bytes 1572868
  168.0 4.0 %copy-start = (f32[16,16384]{1,0:T(8,128)S(1)}, f32[16,16384]{1,0:T(8,128)}, u32[]{:S(2)}) copy-start(f32[16,16384]{1,0:T(8,128)} %get-tuple-element.10) | copy-start | bytes 3145732

commit v6 on v5

--- a/solution.py
+++ b/solution.py
@@ -504,9 +504,9 @@
 
     z_stage(0)
     own_stage(1)
+    z_stage(1)
     own_stage(2)
     loop(model // TILE, token_tile)
-    z_stage(1)
     z_stage(2)
 
     def results(body):

time: 173 us -> 173 us (level)
  no operation moved by 1% of the time
where the time goes in v6:
time: 173 us
  Pallas kernels  164 us (95%)
  local copies, waits for them, and re-layouts  7.17 us (4%)
    pallas_call x1, Pallas kernels, fused(): pl.pallas_call(fused_kernel, out_shape=(jax.ShapeDtypeStruct((rows, model...  164 us
    unnamed x9, local copies, waits for them, and re-layouts  7.17 us

profile of v6, /device:TPU:0, one launch (start us, length us, event | category | flops | bytes accessed | tf_op | source)
XLA Modules:
  0.0 173.0 jit_solution(12466465636844814059)
XLA Ops:
  0.6 0.7 broadcast_multiply_fusion
  1.3 0.8 copy.13
  2.1 0.7 broadcast_add_fusion.ids
  2.8 163.8 %shard_map.102 = (bf16[128,8192]{1,0:T(8,128)(2,1)}, f32[16,8192]{1,0:T(8,128)}, f32[16,16384]{1,0:T(8,128)}, f32[16,512]{1,0:T(8,128)}) custom-call(bf16[128,8192]{1,0:T(8,128)(2,1)} %tok_in.1, bf16[128,16384]{1,0:T(8,128)(2,1)} %gup_in.1, s32[128,2]{1,0:T(8,128)} %broadcast_add_fusion.ids, bf16[16,8192]{1,0:T(8,128)(2,1)} %bitcast.10, ...), custom_call_target="tpu_custom_call" | custom-call | tf_op jit(solution)/shard_map/pallas_call | solution.py:576
  166.6 1.4 copy.14
  168.0 0.0 copy-start.1
  168.0 0.0 copy-start
  168.0 3.2 %copy.18 = bf16[128,8192]{1,0:T(8,128)(2,1)} copy(bf16[128,8192]{1,0:T(8,128)(2,1)} %get-tuple-element.16) | data formatting | bytes 4194304
  171.2 0.0 copy-done.1
  171.2 0.8 copy.19
  172.0 0.0 copy-done
  172.0 1.0 copy.20
Async XLA Ops:
  168.0 3.2 %copy-start.1 = (f32[16,8192]{1,0:T(8,128)S(1)}, f32[16,8192]{1,0:T(8,128)}, u32[]{:S(2)}) copy-start(f32[16,8192]{1,0:T(8,128)} %get-tuple-element.9) | copy-start | bytes 1572868
  168.0 4.0 %copy-start = (f32[16,16384]{1,0:T(8,128)S(1)}, f32[16,16384]{1,0:T(8,128)}, u32[]{:S(2)}) copy-start(f32[16,16384]{1,0:T(8,128)} %get-tuple-element.10) | copy-start | bytes 3145732
